TPU v7x, 512 devices: a whole 4x4x16 slice. The times are simulated.
512 devices in a mesh: domain: 8 (over x, core), fsdp: 64 (over y, z).
Axes of the slice: x: 4, y: 4, z: 16, core: 2. Of those that a mesh axis runs over, the one named last changes fastest.
Arguments:
- gradients: bfloat16 [8, 64, 4096, 512], P('domain', None, 'fsdp')
- row_counts: int32 [64], replicated, may hold values from 2048 to 4096, as said below
- domain_ids: int32 [8], replicated, may hold values from 0 to 7
- domain_weights: float32 [8], replicated, may hold values from 0.2 to 2
Outputs:
- updates: float32 [64, 4096, 512], P('domain', 'fsdp')
- new_weights: float32 [8], replicated
Inputs may be any that keep to these rules, and one draw needn't show every extreme that they name: `row_counts`: each matrix has 4096 or 2048 rows, and both counts occur.
All inputs are finite; a program needn't handle non-finite values.
Results may differ from a plain program's by a relative error of at most 0.0071.
Values may be sent and summed in bfloat16 or wider, within the bound.
A program may use at most 64 MiB of HBM per device.

v0:
```python
import math

import jax
import jax.numpy as jnp
from jax import lax
from jax.sharding import PartitionSpec as P

NS_ITERS = 3
OWNERS = 8


COEF_A = 3.4445
COEF_B = -4.775
COEF_C = 2.0315
MUON_SCALE = 0.2
ETA = 4.0


def partner(shard, axis, stride):
    return lax.ppermute(shard, axis, [(i, i ^ 1 << stride) for i in range(lax.axis_size(axis))])


def group_mixing(domain_ids, domain_weights, kind_count):
    weight_share = domain_weights / jnp.sum(domain_weights)
    onehot = (domain_ids[:, None] == jnp.arange(kind_count, dtype=jnp.int32)[None, :]).astype(
        jnp.float32
    )
    counts = jnp.sum(onehot, axis=0)
    per_member = weight_share / jnp.maximum(counts, 1.0)
    group_mix = jnp.sum(onehot * per_member[None, :], axis=1)
    return (weight_share, onehot, counts, group_mix)


def summed_gram(iterate):
    gram_total = lax.dot_general(
        iterate, iterate, (((0,), (0,)), ((), ())), preferred_element_type=jnp.float32
    )
    for bit_pos in range(OWNERS.bit_length() - 1):
        gram_total = gram_total + partner(gram_total, "fsdp", bit_pos)
    return gram_total


def newton_steps(iterate):
    for repeat in range(NS_ITERS):
        gram_full = lax.optimization_barrier(summed_gram(iterate).astype(jnp.bfloat16))
        square = jnp.dot(gram_full, gram_full, preferred_element_type=jnp.float32)
        poly_term = (COEF_B * gram_full.astype(jnp.float32) + COEF_C * square).astype(jnp.bfloat16)
        iterate = lax.optimization_barrier(
            (
                COEF_A * iterate.astype(jnp.float32)
                + jnp.dot(iterate, poly_term, preferred_element_type=jnp.float32)
            ).astype(jnp.bfloat16)
        )
    return iterate


def share_scores(aligned, squares, norm_slots):
    return lax.psum((aligned, squares, norm_slots), ("domain", "fsdp"))


def body(gradients, row_counts, domain_ids, domain_weights):
    groups = lax.axis_size("domain")
    shards = lax.axis_size("fsdp")
    matrices = row_counts.shape[0]
    rows_src = gradients.shape[2]
    columns = gradients.shape[3]
    per_domain = matrices // groups
    sub_rows = rows_src // OWNERS
    own_rows = shards * sub_rows
    full_rows = rows_src * shards
    domain_pos = lax.axis_index("domain")
    shard_pos = lax.axis_index("fsdp")
    matrix_index = domain_pos * per_domain + shard_pos // OWNERS
    owner_rank = shard_pos % OWNERS
    source = jnp.arange(shards, dtype=jnp.int32)[:, None]
    within = jnp.arange(sub_rows, dtype=jnp.int32)[None, :]
    owner_rows = (source * rows_src + owner_rank * sub_rows + within).reshape(own_rows)
    weight_share, onehot, counts, group_mix = group_mixing(
        domain_ids, domain_weights, domain_weights.shape[0]
    )
    sectioned = gradients.reshape(1, groups, shards, sub_rows, columns)
    received = lax.all_to_all(
        lax.all_to_all(sectioned, "domain", split_axis=1, concat_axis=0, tiled=True),
        "fsdp",
        split_axis=2,
        concat_axis=3,
        tiled=True,
    )
    received = received.reshape(groups, own_rows, columns)
    row_limit = lax.dynamic_index_in_dim(row_counts, matrix_index, 0, keepdims=False)
    row_mask = (owner_rows < row_limit)[None, :, None]
    masked = jnp.where(row_mask, received.astype(jnp.float32), jnp.zeros((), jnp.float32))
    combined = jnp.sum(group_mix[:, None, None] * masked, axis=0)
    aligned = jnp.sum(masked * combined[None], axis=(1, 2))
    squares = jnp.sum(masked * masked, axis=(1, 2))
    own_square = jnp.sum(combined * combined)
    norm_slots = jnp.where(
        jnp.arange(matrices, dtype=jnp.int32) == matrix_index,
        own_square,
        jnp.zeros((), jnp.float32),
    )
    aligned, squares, norm_slots = share_scores(aligned, squares, norm_slots)
    frob_norm = (
        jnp.sqrt(lax.dynamic_index_in_dim(norm_slots, matrix_index, 0, keepdims=False)) + 1e-07
    )
    start_rows = lax.optimization_barrier((combined / frob_norm).astype(jnp.bfloat16))
    finished = newton_steps(start_rows)
    returned = lax.all_to_all(
        finished.reshape(1, shards, sub_rows, columns),
        "fsdp",
        split_axis=1,
        concat_axis=0,
        tiled=True,
    )
    returned = returned.reshape(per_domain, rows_src, columns)
    updates = returned.astype(jnp.float32) * (MUON_SCALE * math.sqrt(full_rows))
    total_sq = jnp.sum(norm_slots)
    cosine = aligned / (jnp.sqrt(squares) * jnp.sqrt(total_sq) + 1e-06)
    score = jnp.sum(onehot * cosine[:, None], axis=0) / jnp.maximum(counts, 1.0)
    raised = weight_share * jnp.exp(ETA * score)
    return (updates, raised / jnp.sum(raised))


def solution(mesh):
    placed = (P("domain", None, "fsdp", None), P(), P(), P())
    return jax.shard_map(
        body,
        mesh=mesh,
        in_specs=placed,
        out_specs=(P("domain", "fsdp", None), P()),
        check_vma=False,
    )
```

profile of v0, /device:TPU:1, one launch (start us, length us, event | category | flops | bytes accessed | tf_op | source)
XLA Modules:
  0.0 935.4 jit_solution(9981151052940490858)
XLA Ops:
  0.6 59.8 %all_to_all.30 = bf16[1,8,64,8,512]{4,3,2,0,1:T(8,128)(2,1)S(1)} all-to-all(bf16[1,8,64,8,512]{4,3,2,0,1:T(8,128)(2,1)} %bitcast.26), channel_id=1, replica_groups=mesh['domain'=8,'fsdp'=64] {'domain'}, dimensions={1} | all-to-all | bytes 8388608 | tf_op jit(solution)/shard_map/all_to_all | solution.py:83
  60.4 2.6 copy.8
  63.0 14.2 %all-to-all-start.1 = ((bf16[8,1,64,8,512]{4,3,0,1,2:T(8,128)(2,1)}), bf16[8,1,64,8,512]{4,3,0,1,2:T(8,128)(2,1)}, u32[]{:S(2)}, u32[]{:S(2)}) async-start(bf16[8,1,64,8,512]{4,3,0,1,2:T(8,128)(2,1)} %copy.8), calls=%async_computation.1 | async-start | bytes 8388608 | tf_op jit(solution)/shard_map/all_to_all | solution.py:82
  80.1 178.7 %all-to-all-done.1 = bf16[8,1,64,8,512]{4,3,0,1,2:T(8,128)(2,1)} async-done(((bf16[8,1,64,8,512]{4,3,0,1,2:T(8,128)(2,1)}), bf16[8,1,64,8,512]{4,3,0,1,2:T(8,128)(2,1)}, u32[]{:S(2)}, u32[]{:S(2)}) %all-to-all-start.1) | async-done | bytes 4194336 | tf_op jit(solution)/shard_map/all_to_all | solution.py:82
  258.8 4.3 multiply_reduce_fusion.2
  264.6 4.3 multiply_reduce_fusion
  268.9 105.8 %all-reduce = (f32[64]{0:T(128)S(1)}, f32[8]{0:T(128)S(1)}, f32[8]{0:T(128)S(1)}) all-reduce(f32[64]{0:T(128)S(1)} %compare_select_fusion, f32[8]{0:T(128)S(1)} %get-tuple-element.3, f32[8]{0:T(128)S(1)} %get-tuple-element.2), channel_id=1, replica_groups=mesh['domain'=8,'fsdp'=64] {'domain','fsdp'}, use_global_device_ids=true, to_apply=%region_5.6 | all-reduce | flops 80 | bytes 640 | tf_op jit(solution)/shard_map/psum | solution.py:58
  376.6 2.9 collective-permute-start
  379.5 22.7 %collective-permute-done = f32[512,512]{1,0:T(8,128)S(1)} collective-permute-done((f32[512,512]{1,0:T(8,128)S(1)}, f32[512,512]{1,0:T(8,128)S(1)}, u32[]{:S(2)}, u32[]{:S(2)}) %collective-permute-start) | collective-permute-done | bytes 1048608 | tf_op jit(solution)/shard_map/ppermute | solution.py:20
  402.4 3.4 collective-permute-start.1
  405.8 45.8 %collective-permute-done.1 = f32[512,512]{1,0:T(8,128)S(1)} collective-permute-done((f32[512,512]{1,0:T(8,128)S(1)}, f32[512,512]{1,0:T(8,128)S(1)}, u32[]{:S(2)}, u32[]{:S(2)}) %collective-permute-start.1) | collective-permute-done | bytes 1048608 | tf_op jit(solution)/shard_map/ppermute | solution.py:20
  451.8 5.8 collective-permute-start.2
  457.6 91.5 %collective-permute-done.2 = f32[512,512]{1,0:T(8,128)S(1)} collective-permute-done((f32[512,512]{1,0:T(8,128)S(1)}, f32[512,512]{1,0:T(8,128)S(1)}, u32[]{:S(2)}, u32[]{:S(2)}) %collective-permute-start.2) | collective-permute-done | bytes 1048608 | tf_op jit(solution)/shard_map/ppermute | solution.py:20
  550.6 1.9 collective-permute-start.3
  552.5 24.2 %collective-permute-done.3 = f32[512,512]{1,0:T(8,128)S(1)} collective-permute-done((f32[512,512]{1,0:T(8,128)S(1)}, f32[512,512]{1,0:T(8,128)S(1)}, u32[]{:S(2)}, u32[]{:S(2)}) %collective-permute-start.3) | collective-permute-done | bytes 1048608 | tf_op jit(solution)/shard_map/ppermute | solution.py:20
  578.8 48.4 %collective-permute-done.4 = f32[512,512]{1,0:T(8,128)S(1)} collective-permute-done((f32[512,512]{1,0:T(8,128)S(1)}, f32[512,512]{1,0:T(8,128)S(1)}, u32[]{:S(2)}, u32[]{:S(2)}) %collective-permute-start.4) | collective-permute-done | bytes 1048608 | tf_op jit(solution)/shard_map/ppermute | solution.py:20
  627.4 2.9 collective-permute-start.5
  630.3 91.9 %collective-permute-done.5 = f32[512,512]{1,0:T(8,128)S(1)} collective-permute-done((f32[512,512]{1,0:T(8,128)S(1)}, f32[512,512]{1,0:T(8,128)S(1)}, u32[]{:S(2)}, u32[]{:S(2)}) %collective-permute-start.5) | collective-permute-done | bytes 1048608 | tf_op jit(solution)/shard_map/ppermute | solution.py:20
  725.7 24.2 %collective-permute-done.6 = f32[512,512]{1,0:T(8,128)S(1)} collective-permute-done((f32[512,512]{1,0:T(8,128)S(1)}, f32[512,512]{1,0:T(8,128)S(1)}, u32[]{:S(2)}, u32[]{:S(2)}) %collective-permute-start.6) | collective-permute-done | bytes 1048608 | tf_op jit(solution)/shard_map/ppermute | solution.py:20
  752.1 48.4 %collective-permute-done.7 = f32[512,512]{1,0:T(8,128)S(1)} collective-permute-done((f32[512,512]{1,0:T(8,128)S(1)}, f32[512,512]{1,0:T(8,128)S(1)}, u32[]{:S(2)}, u32[]{:S(2)}) %collective-permute-start.7) | collective-permute-done | bytes 1048608 | tf_op jit(solution)/shard_map/ppermute | solution.py:20
  800.6 2.5 collective-permute-start.8
  803.1 92.0 %collective-permute-done.8 = f32[512,512]{1,0:T(8,128)S(1)} collective-permute-done((f32[512,512]{1,0:T(8,128)S(1)}, f32[512,512]{1,0:T(8,128)S(1)}, u32[]{:S(2)}, u32[]{:S(2)}) %collective-permute-start.8) | collective-permute-done | bytes 1048608 | tf_op jit(solution)/shard_map/ppermute | solution.py:20
  896.9 8.0 all-to-all-start.2
  909.0 25.4 %all-to-all-done.2 = bf16[1,64,8,512]{3,2,0,1:T(8,128)(2,1)S(1)} async-done(((bf16[1,64,8,512]{3,2,0,1:T(8,128)(2,1)}), bf16[1,64,8,512]{3,2,0,1:T(8,128)(2,1)S(1)}, u32[]{:S(2)}, u32[]{:S(2)}) %all-to-all-start.2) | async-done | bytes 524320 | tf_op jit(solution)/shard_map/all_to_all | solution.py:108
  (41 shorter events, 21.8 us)
Async XLA Ops:
  63.0 14.2 %copy-start = (f32[8]{0:T(128)S(1)}, f32[8]{0:T(128)}, u32[]{:S(2)}) copy-start(f32[8]{0:T(128)} %param.7) | copy-start | bytes 100
  63.0 14.8 %copy-start.1 = (s32[64]{0:T(128)S(1)}, s32[64]{0:T(128)}, u32[]{:S(2)}) copy-start(s32[64]{0:T(128)} %param.5) | copy-start | bytes 772
  63.0 15.4 %copy-start.2 = (s32[8]{0:T(128)S(1)}, s32[8]{0:T(128)}, u32[]{:S(2)}) copy-start(s32[8]{0:T(128)} %param.6) | copy-start | bytes 100
  63.0 195.8 %all-to-all-start.1 = ((bf16[8,1,64,8,512]{4,3,0,1,2:T(8,128)(2,1)}), bf16[8,1,64,8,512]{4,3,0,1,2:T(8,128)(2,1)}, u32[]{:S(2)}, u32[]{:S(2)}) async-start(bf16[8,1,64,8,512]{4,3,0,1,2:T(8,128)(2,1)} %copy.8), calls=%async_computation.1 | async-start | bytes 8388608 | tf_op jit(solution)/shard_map/all_to_all | solution.py:82
  376.6 25.6 %collective-permute-start = (f32[512,512]{1,0:T(8,128)S(1)}, f32[512,512]{1,0:T(8,128)S(1)}, u32[]{:S(2)}, u32[]{:S(2)}) collective-permute-start(f32[512,512]{1,0:T(8,128)S(1)} %fusion.17), channel_id=1, source_target_pairs={{0,1},{1,0},{2,3},{3,2},{4,5},{5,4},{6,7},{7,6},{8,9},{9,8},{10,11... | collective-permute-start | bytes 3145736 | tf_op jit(solution)/shard_map/ppermute | solution.py:20
  402.4 49.2 %collective-permute-start.1 = (f32[512,512]{1,0:T(8,128)S(1)}, f32[512,512]{1,0:T(8,128)S(1)}, u32[]{:S(2)}, u32[]{:S(2)}) collective-permute-start(f32[512,512]{1,0:T(8,128)S(1)} %add.113), channel_id=1, source_target_pairs={{0,2},{1,3},{2,0},{3,1},{4,6},{5,7},{6,4},{7,5},{8,10},{9,11},{10,... | collective-permute-start | bytes 3145736 | tf_op jit(solution)/shard_map/ppermute | solution.py:20
  451.8 97.3 %collective-permute-start.2 = (f32[512,512]{1,0:T(8,128)S(1)}, f32[512,512]{1,0:T(8,128)S(1)}, u32[]{:S(2)}, u32[]{:S(2)}) collective-permute-start(f32[512,512]{1,0:T(8,128)S(1)} %add.114), channel_id=1, source_target_pairs={{0,4},{1,5},{2,6},{3,7},{4,0},{5,1},{6,2},{7,3},{8,12},{9,13},{10,... | collective-permute-start | bytes 3145736 | tf_op jit(solution)/shard_map/ppermute | solution.py:20
  550.6 26.1 %collective-permute-start.3 = (f32[512,512]{1,0:T(8,128)S(1)}, f32[512,512]{1,0:T(8,128)S(1)}, u32[]{:S(2)}, u32[]{:S(2)}) collective-permute-start(f32[512,512]{1,0:T(8,128)S(1)} %fusion.18), channel_id=1, source_target_pairs={{0,1},{1,0},{2,3},{3,2},{4,5},{5,4},{6,7},{7,6},{8,9},{9,8},{10,11... | collective-permute-start | bytes 3145736 | tf_op jit(solution)/shard_map/ppermute | solution.py:20
  576.9 50.3 %collective-permute-start.4 = (f32[512,512]{1,0:T(8,128)S(1)}, f32[512,512]{1,0:T(8,128)S(1)}, u32[]{:S(2)}, u32[]{:S(2)}) collective-permute-start(f32[512,512]{1,0:T(8,128)S(1)} %add.118), channel_id=1, source_target_pairs={{0,2},{1,3},{2,0},{3,1},{4,6},{5,7},{6,4},{7,5},{8,10},{9,11},{10,... | collective-permute-start | bytes 3145736 | tf_op jit(solution)/shard_map/ppermute | solution.py:20
  627.4 94.9 %collective-permute-start.5 = (f32[512,512]{1,0:T(8,128)S(1)}, f32[512,512]{1,0:T(8,128)S(1)}, u32[]{:S(2)}, u32[]{:S(2)}) collective-permute-start(f32[512,512]{1,0:T(8,128)S(1)} %add.119), channel_id=1, source_target_pairs={{0,4},{1,5},{2,6},{3,7},{4,0},{5,1},{6,2},{7,3},{8,12},{9,13},{10,... | collective-permute-start | bytes 3145736 | tf_op jit(solution)/shard_map/ppermute | solution.py:20
  723.8 26.1 %collective-permute-start.6 = (f32[512,512]{1,0:T(8,128)S(1)}, f32[512,512]{1,0:T(8,128)S(1)}, u32[]{:S(2)}, u32[]{:S(2)}) collective-permute-start(f32[512,512]{1,0:T(8,128)S(1)} %fusion.19), channel_id=1, source_target_pairs={{0,1},{1,0},{2,3},{3,2},{4,5},{5,4},{6,7},{7,6},{8,9},{9,8},{10,11... | collective-permute-start | bytes 3145736 | tf_op jit(solution)/shard_map/ppermute | solution.py:20
  750.1 50.3 %collective-permute-start.7 = (f32[512,512]{1,0:T(8,128)S(1)}, f32[512,512]{1,0:T(8,128)S(1)}, u32[]{:S(2)}, u32[]{:S(2)}) collective-permute-start(f32[512,512]{1,0:T(8,128)S(1)} %add.123), channel_id=1, source_target_pairs={{0,2},{1,3},{2,0},{3,1},{4,6},{5,7},{6,4},{7,5},{8,10},{9,11},{10,... | collective-permute-start | bytes 3145736 | tf_op jit(solution)/shard_map/ppermute | solution.py:20
  800.6 94.5 %collective-permute-start.8 = (f32[512,512]{1,0:T(8,128)S(1)}, f32[512,512]{1,0:T(8,128)S(1)}, u32[]{:S(2)}, u32[]{:S(2)}) collective-permute-start(f32[512,512]{1,0:T(8,128)S(1)} %add.124), channel_id=1, source_target_pairs={{0,4},{1,5},{2,6},{3,7},{4,0},{5,1},{6,2},{7,3},{8,12},{9,13},{10,... | collective-permute-start | bytes 3145736 | tf_op jit(solution)/shard_map/ppermute | solution.py:20
  896.9 37.4 %all-to-all-start.2 = ((bf16[1,64,8,512]{3,2,0,1:T(8,128)(2,1)}), bf16[1,64,8,512]{3,2,0,1:T(8,128)(2,1)S(1)}, u32[]{:S(2)}, u32[]{:S(2)}) async-start(bf16[1,64,8,512]{3,2,0,1:T(8,128)(2,1)} %bitcast.6), calls=%async_computation.2 | async-start | bytes 1048576 | tf_op jit(solution)/shard_map/all_to_all | solution.py:108
where the time goes:
time: 938 us; the launch traced here: 935 us
  waiting for transfers between devices  693 us (74%)
  blocking collectives  166 us (18%)
  starting transfers between devices  47.4 us (5%)
  other arithmetic  18.9 us (2%)
    ppermute x9, waiting for transfers between devices, partner(): lax.ppermute(shard, axis, [(i, i ^ 1 << stride) for i in range(lax.axis_s...  489 us
    all_to_all x1, waiting for transfers between devices, body(): lax.all_to_all(lax.all_to_all(sectioned, 'domain', split_axis=1, concat_a...  179 us
    psum x1, blocking collectives, share_scores(): return lax.psum((aligned, squares, norm_slots), ('domain', 'fsdp'))  106 us
    all_to_all x1, blocking collectives, body(): lax.all_to_all(sectioned, 'domain', split_axis=1, concat_axis=0, tiled=True)  59.8 us
    all_to_all x1, waiting for transfers between devices, body(): lax.all_to_all(finished.reshape(1, shards, sub_rows, columns), 'fsdp', sp...  25.4 us
    ppermute x9, starting transfers between devices, partner(): lax.ppermute(shard, axis, [(i, i ^ 1 << stride) for i in range(lax.axis_s...  25.2 us
  transfers between devices with their start and end apart: 11, of which 11 were waited for; matrix products, arithmetic and copies ran while one was open for 1% of the time, Pallas kernels for 0%

commit v1 on v0

v1 whole, which is shorter than its diff:
```python
import functools
import math

import jax
import jax.numpy as jnp
from jax import lax
from jax.experimental import pallas as pl
from jax.experimental.pallas import tpu as pltpu
from jax.sharding import PartitionSpec as P

COEF_A = 3.4445
COEF_B = -4.775
COEF_C = 2.0315
MUON_SCALE = 0.2
ETA = 4.0
F32 = jnp.float32
BF16 = jnp.bfloat16
CORES = 2
RING = 4


def owner_position(slot, core, y_size, z_size):
    if y_size * z_size != 64:
        return (slot + core) % (y_size * z_size)
    quad, half = slot % 4, slot // 4
    z_pos = 4 * quad + 2 * half + core
    y_pos = (quad + ((0, 2), (1, 0))[half][core]) % 4
    return y_pos * z_size + z_pos


def kernel(
    sizes,
    counts_ref, ids_ref, weights_ref, grads_ref,
    out_ref, new_ref,
    own, sib, far_out, near_out, far_in, near_in, comb, rows, done,
    gram, term, lin0, lin1, gram_b, term_b, lin0_b, lin1_b, score, sq_acc,
    own_sem, sib_send, sib_recv, far_send, far_recv, near_send, near_recv,
    ag_send, ag_recv, agf_send, agf_recv, in_send, in_recv, out_send, out_recv,
    red_send, red_recv,
):
    groups, y_size, z_size, mats, height, width = sizes
    shards = y_size * z_size
    pair = mats // 4
    d = lax.axis_index("domain")
    f = lax.axis_index("fsdp")
    x, core = d // CORES, d % CORES
    y, z = f // z_size, f % z_size
    sibling = CORES * x + (1 - core)
    ring = [(x + step) % RING for step in (2, 1, 3, 0)]
    plus, minus = CORES * ring[1] + core, CORES * ring[2] + core
    owners = [
        jnp.where(
            core == 0,
            owner_position(j, 0, y_size, z_size),
            owner_position(j, 1, y_size, z_size),
        )
        for j in range(mats)
    ]
    own_slot = jnp.int32(0)
    owned = jnp.int32(0)
    for j in range(mats):
        own_slot = jnp.where(f == owners[j], j, own_slot)
        owned = jnp.where(f == owners[j], 1, owned)
    is_owner = owned == 1

    def remote(src, dst, send, recv, dd, ff):
        return pltpu.make_async_remote_copy(
            src_ref=src, dst_ref=dst, send_sem=send, recv_sem=recv,
            device_id=(dd, ff), device_id_type=pl.DeviceIdType.MESH,
        )

    def block(ref, first, count=1):
        return ref.at[pl.ds(first * height, count * height)]

    barrier = pltpu.get_barrier_semaphore()

    def greet(dd, ff):
        pl.semaphore_signal(
            barrier, inc=1, device_id=(dd, ff), device_id_type=pl.DeviceIdType.MESH
        )

    half = mats // 2

    def own_copy(rel, stage):
        first = mats * (CORES * ring[rel] + core) + half * stage
        return pltpu.make_async_copy(
            block(grads_ref, first, half),
            block(own, rel * mats + half * stage, half),
            own_sem.at[rel, stage],
        )

    def sib_copy(rel, stage):
        first = mats * (CORES * ring[rel] + (1 - core)) + half * stage
        return remote(
            block(grads_ref, first, half),
            block(sib, rel * mats + half * stage, half),
            sib_send.at[rel, stage], sib_recv.at[rel, stage], sibling, f,
        )

    order = [(0, 0), (1, 0), (2, 0), (0, 1), (3, 0), (1, 1), (2, 1), (3, 1)]
    for rel, stage in order:
        own_copy(rel, stage).start()

    for step in range(1, groups):
        greet((d + step) % groups, f)
    for step in range(1, y_size):
        greet(d, (y + step) % y_size * z_size + z)
    for step in range(1, z_size):
        greet(d, y * z_size + (z + step) % z_size)
    for j in range(mats):

        @pl.when(f != owners[j])
        def _():
            greet(d, owners[j])

    @pl.when(is_owner)
    def _():
        def one(step, carry):
            greet(d, (f + step) % shards)
            return carry

        lax.fori_loop(1, shards, one, 0)

    pl.semaphore_wait(
        barrier,
        (groups - 1) + (y_size - 1) + (z_size - 1) + mats - owned + owned * (shards - 1),
    )

    for rel, stage in order:
        sib_copy(rel, stage).start()

    total_weight = weights_ref[0]
    for k in range(1, groups):
        total_weight = total_weight + weights_ref[k]

    def mix_row(group):
        kind = ids_ref[group]
        count = jnp.float32(0)
        for h in range(groups):
            count = count + jnp.where(ids_ref[h] == kind, 1.0, 0.0)
        full = lambda value: jnp.full((1, width), value, F32)
        return full(weights_ref[kind]) / full(total_weight) / jnp.maximum(full(count), 1.0)

    mix_own, mix_sib = mix_row(d), mix_row(sibling)

    def keep(rel, j):
        index = mats * (CORES * ring[rel] + core) + j
        return jnp.where(f * height < counts_ref[index], 1.0, 0.0)

    def partial(rel, j):
        at = pl.ds((rel * mats + j) * height, height)
        kept = keep(rel, j)
        return (mix_own * kept) * own[at, :].astype(F32) + (mix_sib * kept) * sib[
            at, :
        ].astype(F32)

    def arrived(rel, stage):
        own_copy(rel, stage).wait()
        sib_copy(rel, stage).wait_recv()

    def far_copy(way, stage):
        part = way * 2 + stage
        return remote(
            block(far_out, part * pair, pair), block(far_in, part * pair, pair),
            far_send.at[part], far_recv.at[part], (plus, minus)[way], f,
        )

    def near_copy(way, quarter):
        first = way * mats + quarter * pair
        return remote(
            block(near_out, first, pair), block(near_in, first, pair),
            near_send.at[way, quarter], near_recv.at[way, quarter], (plus, minus)[way], f,
        )

    def send_far(stage):
        arrived(0, stage)
        for way in (0, 1):
            for i in range(pair):
                at = pl.ds(((way * 2 + stage) * pair + i) * height, height)
                far_out[at, :] = partial(0, (2 * stage + way) * pair + i).astype(BF16)
            far_copy(way, stage).start()

    def send_near(stage):
        for way in (0, 1):
            arrived(1 + way, stage)
            quarter = 2 * stage + 1 - way
            for i in range(pair):
                j = quarter * pair + i
                at = pl.ds((way * mats + j) * height, height)
                near_out[at, :] = partial(1 + way, j).astype(BF16)
            near_copy(way, quarter).start()

    def send_merged(stage):
        for way in (0, 1):
            far_copy(way, stage).wait_recv()
            quarter = 2 * stage + way
            for i in range(pair):
                j = quarter * pair + i
                at = pl.ds((way * mats + j) * height, height)
                came = pl.ds(((way * 2 + stage) * pair + i) * height, height)
                near_out[at, :] = (
                    partial(1 + way, j) + far_in[came, :].astype(F32)
                ).astype(BF16)
            near_copy(way, quarter).start()

    slot_here = z * y_size + y

    def in_copy(j):
        return remote(
            block(comb, 3 * mats + j), block(rows, slot_here),
            in_send.at[j], in_recv.at[z], d, owners[j],
        )

    def combine(stage):
        arrived(3, stage)
        for quarter in (2 * stage, 2 * stage + 1):
            for way in (0, 1):
                near_copy(way, quarter).wait_recv()
            for i in range(pair):
                j = quarter * pair + i
                left = pl.ds(j * height, height)
                right = pl.ds((mats + j) * height, height)
                value = partial(3, j) + (
                    near_in[left, :].astype(F32) + near_in[right, :].astype(F32)
                )
                sq_acc[...] += jnp.sum(
                    (value * value).reshape(height // 8, 8, width), axis=0
                )
                comb[pl.ds((3 * mats + j) * height, height), :] = value.astype(BF16)

                @pl.when(f != owners[j])
                def _():
                    in_copy(j).start()

                @pl.when(f == owners[j])
                def _():
                    pltpu.make_async_copy(
                        block(comb, 3 * mats + j), block(rows, slot_here), in_recv.at[z]
                    ).start()

    sq_acc[...] = jnp.zeros_like(sq_acc)
    send_far(0)
    send_near(0)
    send_far(1)
    send_merged(0)
    send_near(1)
    combine(0)
    send_merged(1)
    combine(1)

    def ag_copy(way, quarter):
        first = quarter * pair
        return remote(
            block(comb, 3 * mats + first, pair),
            block(comb, (2, 1)[way] * mats + first, pair),
            ag_send.at[way, quarter], ag_recv.at[way, quarter], (plus, minus)[way], f,
        )

    def agf_copy(way, stage):
        first = (2 * stage + way) * pair
        return remote(
            block(comb, (2, 1)[way] * mats + first, pair), block(comb, first, pair),
            agf_send.at[way, stage], agf_recv.at[way, stage], (plus, minus)[way], f,
        )

    for quarter in range(4):
        for way in (0, 1):
            ag_copy(way, quarter).start()

    band = y_size * height

    def near_z(step):
        shift = jnp.where(step % 2 == 1, (step + 1) // 2, z_size - step // 2)
        return (z + shift) % z_size

    @pl.when(is_owner)
    def _():
        gram[...] = jnp.zeros_like(gram)

        def one(step, carry):
            zz = near_z(step)
            here = rows.at[pl.ds(zz * band, band)]
            pltpu.make_async_copy(here, here, in_recv.at[zz]).wait()
            part = here[...]
            gram[...] += lax.dot_general(
                part, part, (((0,), (0,)), ((), ())), preferred_element_type=F32
            )
            return carry

        lax.fori_loop(0, z_size, one, 0)

    for stage in (0, 1):
        for way in (0, 1):
            ag_copy(way, 2 * stage + way).wait_recv()
            agf_copy(way, stage).start()

    def out_copy(y_to, z_to):
        slot = z_to * y_size + y_to
        return remote(
            block(done, slot), block(out_ref, own_slot),
            out_send.at[slot], out_recv.at[own_slot], d, y_to * z_size + z_to,
        )

    @pl.when(is_owner)
    def _():
        row_id = lax.broadcasted_iota(jnp.int32, (width, width), 0)
        col_id = lax.broadcasted_iota(jnp.int32, (width, width), 1)
        trace = jnp.sum(jnp.where(row_id == col_id, gram[...], 0.0), axis=0, keepdims=True)
        trace = jnp.sum(trace, axis=1, keepdims=True)
        scale = 1.0 / (jnp.sqrt(trace) + 1e-07)
        dot = lambda a, b: jnp.dot(a[...], b[...], preferred_element_type=F32)

        gram[...] = gram[...] * scale * scale
        gram_b[...] = gram[...].astype(BF16)
        for lin, lin_b in ((lin0, lin0_b), (lin1, lin1_b)):
            lin[...] = COEF_B * gram[...] + COEF_C * dot(gram_b, gram_b)
            lin_b[...] = lin[...].astype(BF16)
            term[...] = COEF_A * gram[...] + dot(lin_b, gram_b)
            term_b[...] = term[...].astype(BF16)
            gram[...] = COEF_A * term[...] + dot(lin_b, term_b)
            gram_b[...] = gram[...].astype(BF16)
        lin0[...] = COEF_A * (lin0[...] + lin1[...]) + dot(lin0_b, lin1_b)
        lin0_b[...] = lin0[...].astype(BF16)
        lin1[...] = COEF_B * gram[...] + COEF_C * dot(gram_b, gram_b)
        lin1_b[...] = lin1[...].astype(BF16)
        whole = COEF_A**2 * lin1[...] + COEF_A * lin0[...] + dot(lin0_b, lin1_b)
        whole = whole + jnp.where(row_id == col_id, COEF_A**3, 0.0)
        gram_b[...] = (whole * scale).astype(BF16)

        def one(step, carry):
            zz = near_z(z_size - 1 - step)
            at = pl.ds(zz * band, band)
            done[at, :] = jnp.dot(
                rows[at, :], gram_b[...], preferred_element_type=F32
            ).astype(BF16)
            for y_to in range(y_size):
                here = y_to * z_size + zz == f

                @pl.when(jnp.logical_not(here))
                def _():
                    out_copy(y_to, zz).start()

                @pl.when(here)
                def _():
                    pltpu.make_async_copy(
                        block(done, slot_here), block(out_ref, own_slot),
                        out_recv.at[own_slot],
                    ).start()

            return carry

        lax.fori_loop(0, z_size, one, 0)

    for way in (0, 1):
        for quarter in range(4):
            if quarter % 2 != way:
                ag_copy(way, quarter).wait_recv()
        for stage in (0, 1):
            agf_copy(way, stage).wait_recv()

    fold = lambda value: jnp.sum(value.reshape(height // 8, 8, width), axis=0)

    def align(index, carry):
        rel, j = index // mats, index % mats
        step = jnp.where(rel == 0, 2, jnp.where(rel == 1, 1, jnp.where(rel == 2, 3, 0)))
        matrix = mats * (CORES * ((x + step) % RING) + core) + j
        kept = jnp.where(f * height < counts_ref[matrix], 1.0, 0.0)
        at = pl.ds(index * height, height)
        mine, other = own[at, :].astype(F32), sib[at, :].astype(F32)
        both = comb[at, :].astype(F32)
        return (
            carry[0] + fold(mine * both),
            carry[1] + fold(other * both),
            carry[2] + kept * fold(mine * mine),
            carry[3] + kept * fold(other * other),
        )

    empty = jnp.zeros((8, width), F32)
    sums = lax.fori_loop(0, RING * mats, align, (empty,) * 4)
    sums = [
        jnp.sum(jnp.sum(value, axis=0, keepdims=True), axis=1, keepdims=True)
        for value in (*sums, sq_acc[...])
    ]
    sub = lax.broadcasted_iota(jnp.int32, (8, 128), 0)
    lane = lax.broadcasted_iota(jnp.int32, (8, 128), 1)

    def by_group(mine, other):
        return jnp.where(sub == d, mine, jnp.where(sub == sibling, other, 0.0))

    tile = jnp.where(
        lane == 0,
        by_group(sums[0], sums[1]),
        jnp.where(
            lane == 1,
            by_group(sums[2], sums[3]),
            jnp.where(lane == 2, sums[4], 0.0),
        ),
    )
    base = 0
    for size, place, where in (
        (groups, d, lambda to: (to, f)),
        (y_size, y, lambda to: (d, to * z_size + z)),
        (z_size, z, lambda to: (d, y * z_size + to)),
    ):
        score[base + place] = tile

        def red_copy(step, base=base, size=size, place=place, where=where):
            return remote(
                score.at[base + place], score.at[base + place],
                red_send.at[base + step], red_recv.at[base + place],
                *where((place + step) % size),
            )

        def red_wait(step, base=base, size=size, place=place):
            came = score.at[base + (place + step) % size]
            pltpu.make_async_copy(
                came, came, red_recv.at[base + (place + step) % size]
            ).wait()

        for step in range(1, size):
            red_copy(step).start()
        for step in range(1, size):
            red_wait(step)
        tile = score[base]
        for i in range(1, size):
            tile = tile + score[base + i]
        for step in range(1, size):
            red_copy(step).wait_send()
        base += size

    id_col = jnp.zeros((8, 128), jnp.int32)
    weight_row = jnp.zeros((1, 128), F32)
    for g in range(groups):
        id_col = jnp.where(sub == g, ids_ref[g], id_col)
        weight_row = jnp.where(lane[:1] == g, weights_ref[g], weight_row)
    column = lambda k: jnp.sum(jnp.where(lane == k, tile, 0.0), axis=1, keepdims=True)
    aligned, squares, total_sq = column(0), column(1), column(2)
    cosine = aligned / (jnp.sqrt(squares) * jnp.sqrt(total_sq) + 1e-06)
    onehot = jnp.where(id_col == lane, 1.0, 0.0)
    kind_counts = jnp.sum(onehot, axis=0, keepdims=True)
    points = jnp.sum(onehot * cosine, axis=0, keepdims=True) / jnp.maximum(kind_counts, 1.0)
    share = weight_row / jnp.full((1, 128), total_weight, F32)
    raised = share * jnp.exp(ETA * points)
    new_ref[...] = raised / jnp.sum(raised, axis=1, keepdims=True)

    for rel, stage in order:
        sib_copy(rel, stage).wait_send()
    for way in (0, 1):
        for stage in (0, 1):
            far_copy(way, stage).wait_send()
            agf_copy(way, stage).wait_send()
        for quarter in range(4):
            near_copy(way, quarter).wait_send()
            ag_copy(way, quarter).wait_send()
    for j in range(mats):

        @pl.when(f != owners[j])
        def _():
            in_copy(j).wait_send()

    @pl.when(is_owner)
    def _():
        def one(step, carry):
            slot = (slot_here + step) % shards
            out_copy(slot % y_size, slot // y_size).wait_send()
            return carry

        lax.fori_loop(1, shards, one, 0)

    for j in range(mats):
        here = block(out_ref, j)
        pltpu.make_async_copy(here, here, out_recv.at[j]).wait()


def body(gradients, row_counts, domain_ids, domain_weights):
    groups = lax.axis_size("domain")
    shards = lax.axis_size("fsdp")
    matrices, height, width = gradients.shape[1:]
    mats = matrices // groups
    y_size = 4 if shards == 64 else 2
    z_size = shards // y_size
    sizes = (groups, y_size, z_size, mats, height, width)
    assert groups == CORES * RING
    block = lambda count: pltpu.VMEM((count * height, width), BF16)
    square = lambda dtype: pltpu.VMEM((width, width), dtype)
    dma = lambda *shape: pltpu.SemaphoreType.DMA(shape)
    red = groups + y_size + z_size
    finished, new_weights = pl.pallas_call(
        functools.partial(kernel, sizes),
        out_shape=(
            jax.ShapeDtypeStruct((mats * height, width), BF16),
            jax.ShapeDtypeStruct((1, 128), F32),
        ),
        in_specs=[pl.BlockSpec(memory_space=pltpu.SMEM)] * 3
        + [pl.BlockSpec(memory_space=pl.ANY)],
        out_specs=(
            pl.BlockSpec(memory_space=pl.ANY),
            pl.BlockSpec(memory_space=pltpu.VMEM),
        ),
        scratch_shapes=[
            block(RING * mats), block(RING * mats), block(mats), block(2 * mats),
            block(mats), block(2 * mats), block(RING * mats), block(shards), block(shards),
            square(F32), square(F32), square(F32), square(F32),
            square(BF16), square(BF16), square(BF16), square(BF16),
            pltpu.VMEM((red, 8, 128), F32), pltpu.VMEM((8, width), F32),
            dma(4, 2), dma(4, 2), dma(4, 2), dma(4), dma(4), dma(2, 4), dma(2, 4),
            dma(2, 4), dma(2, 4), dma(2, 2), dma(2, 2), dma(mats), dma(z_size),
            dma(shards), dma(mats), dma(red), dma(red),
        ],
        compiler_params=pltpu.CompilerParams(
            collective_id=0, has_side_effects=True, vmem_limit_bytes=48 * 2**20
        ),
        cost_estimate=pl.CostEstimate(
            flops=20 * 10**9, bytes_accessed=8 * 2**20, transcendentals=0
        ),
    )(row_counts, domain_ids, domain_weights, gradients.reshape(matrices * height, width))
    full_rows = height * shards
    updates = finished.reshape(mats, height, width).astype(F32) * (
        MUON_SCALE * math.sqrt(full_rows)
    )
    return (updates, new_weights[0, :groups])


def solution(mesh):
    placed = (P("domain", None, "fsdp", None), P(), P(), P())
    return jax.shard_map(
        body,
        mesh=mesh,
        in_specs=placed,
        out_specs=(P("domain", "fsdp", None), P()),
        check_vma=False,
    )
```

time: 938 us -> 133 us (0.14)
  waiting for transfers between devices: 693 us -> 0 us
  blocking collectives: 166 us -> 0 us
  Pallas kernels: 0 us -> 126 us
  starting transfers between devices: 47.4 us -> 0 us
  other arithmetic: 18.9 us -> 1.11 us
    ppermute x9 -> x0, waiting for transfers between devices: 489 us -> none  [partner(): lax.ppermute(shard, axis, [(i, i ^ 1 << stride) for i in range(lax.axis_s...]
    all_to_all x2 -> x0, waiting for transfers between devices: 204 us -> none  [the longest x1 179 us: body(): lax.all_to_all(lax.all_to_all(sectioned, 'domain', split_axis=1, concat_a...]
    pallas_call x0 -> x1, Pallas kernels: none -> 126 us  [body(): pl.pallas_call(functools.partial(kernel, sizes), out_shape=(jax.ShapeDtyp...]
    psum x1 -> x0, blocking collectives: 106 us -> none  [share_scores(): return lax.psum((aligned, squares, norm_slots), ('domain', 'fsdp'))]
    all_to_all x1 -> x0, blocking collectives: 59.8 us -> none  [body(): lax.all_to_all(sectioned, 'domain', split_axis=1, concat_axis=0, tiled=True)]
    ppermute x9 -> x0, starting transfers between devices: 25.2 us -> none  [partner(): lax.ppermute(shard, axis, [(i, i ^ 1 << stride) for i in range(lax.axis_s...]
    all_to_all x2 -> x0, starting transfers between devices: 22.1 us -> none  [the longest x1 14.2 us: body(): lax.all_to_all(lax.all_to_all(sectioned, 'domain', split_axis=1, concat_a...]
    reduce_sum x9 -> x0, other arithmetic: 12.4 us -> none  [the longest x1 4.32 us: body(): combined = jnp.sum(group_mix[:, None, None] * masked, axis=0)]
  transfers between devices with their start and end apart: 11 -> 0, of which waited for: 11 -> 0; matrix products, arithmetic and copies ran while one was open for 1% -> 0% of each run, Pallas kernels for 0% -> 0%
where the time goes in v1:
time: 133 us
  Pallas kernels  126 us (95%)
  local copies, waits for them, and re-layouts  4.66 us (4%)
    pallas_call x1, Pallas kernels, body(): pl.pallas_call(functools.partial(kernel, sizes), out_shape=(jax.ShapeDtyp...  126 us
    unnamed x8, local copies, waits for them, and re-layouts  4.15 us

profile of v1, /device:TPU:1, one launch (start us, length us, event | category | flops | bytes accessed | tf_op | source)
XLA Modules:
  0.0 132.8 jit_solution(13393045644943820027)
XLA Ops:
  0.6 0.0 copy-start
  0.6 2.2 %copy-done = bf16[1,64,64,512]{3,2,1,0:T(8,128)(2,1)S(1)} copy-done((bf16[1,64,64,512]{3,2,1,0:T(8,128)(2,1)S(1)}, bf16[1,64,64,512]{3,2,1,0:T(8,128)(2,1)}, u32[]{:S(2)}) %copy-start) | copy-done | bytes 4194328
  2.8 0.0 copy-start.1
  2.8 0.7 copy-done.1
  3.5 0.0 copy-start.2
  3.5 0.7 copy-done.2
  4.1 0.0 copy-start.3
  4.1 0.7 copy-done.3
  4.8 126.4 %shard_map.59 = (bf16[512,512]{1,0:T(8,128)(2,1)S(1)}, f32[1,128]{1,0:T(1,128)S(1)}) custom-call(s32[64]{0:T(128)S(1)} %copy-done.1, s32[8]{0:T(128)S(1)} %copy-done.2, f32[8]{0:T(128)S(1)} %copy-done.3, bf16[4096,512]{1,0:T(8,128)(2,1)S(1)} %bitcast.4), custom_call_target="tpu_custom_call" | custom-call | flops 20000000000 | bytes 8388608 | tf_op jit(solution)/shard_map/pallas_call | solution.py:488
  131.2 0.5 slice_bitcast_fusion
  131.7 1.1 convert_multiply_fusion
Async XLA Ops:
  0.6 2.2 %copy-start = (bf16[1,64,64,512]{3,2,1,0:T(8,128)(2,1)S(1)}, bf16[1,64,64,512]{3,2,1,0:T(8,128)(2,1)}, u32[]{:S(2)}) copy-start(bf16[1,64,64,512]{3,2,1,0:T(8,128)(2,1)} %param.4) | copy-start | bytes 12582916
  2.8 0.7 copy-start.1
  3.5 0.7 copy-start.2
  4.1 0.7 copy-start.3

commit v2 on v1

--- a/solution.py
+++ b/solution.py
@@ -21,7 +21,7 @@
 
 def owner_position(slot, core, y_size, z_size):
     if y_size * z_size != 64:
-        return (slot + core) % (y_size * z_size)
+        return CORES * slot + core
     quad, half = slot % 4, slot // 4
     z_pos = 4 * quad + 2 * half + core
     y_pos = (quad + ((0, 2), (1, 0))[half][core]) % 4
@@ -33,35 +33,42 @@
     counts_ref, ids_ref, weights_ref, grads_ref,
     out_ref, new_ref,
     own, sib, far_out, near_out, far_in, near_in, comb, rows, done,
-    gram, term, lin0, lin1, gram_b, term_b, lin0_b, lin1_b, score, sq_acc,
+    gram, gram_in, term, lin0, lin1, gram_b, term_b, lin0_b, lin1_b, score, sq_acc,
     own_sem, sib_send, sib_recv, far_send, far_recv, near_send, near_recv,
     ag_send, ag_recv, agf_send, agf_recv, in_send, in_recv, out_send, out_recv,
-    red_send, red_recv,
+    red_send, red_recv, swap_send, swap_recv, known,
 ):
-    groups, y_size, z_size, mats, height, width = sizes
-    shards = y_size * z_size
+    groups, y_size, z_size, z_low, mats, height, width = sizes
+    z_high = z_size // z_low
+    bands = z_size // CORES
     pair = mats // 4
     d = lax.axis_index("domain")
     f = lax.axis_index("fsdp")
     x, core = d // CORES, d % CORES
     y, z = f // z_size, f % z_size
+    zh, zl = z // z_low, z % z_low
     sibling = CORES * x + (1 - core)
     ring = [(x + step) % RING for step in (2, 1, 3, 0)]
     plus, minus = CORES * ring[1] + core, CORES * ring[2] + core
-    owners = [
-        jnp.where(
-            core == 0,
+    def owner(j, of_core):
+        return jnp.where(
+            of_core == 0,
             owner_position(j, 0, y_size, z_size),
             owner_position(j, 1, y_size, z_size),
         )
-        for j in range(mats)
-    ]
+
+    owners = [owner(j, core) for j in range(mats)]
     own_slot = jnp.int32(0)
     owned = jnp.int32(0)
+    role = jnp.int32(0)
     for j in range(mats):
-        own_slot = jnp.where(f == owners[j], j, own_slot)
-        owned = jnp.where(f == owners[j], 1, owned)
+        first, second = f == owners[j], f == owner(j, 1 - core)
+        either = jnp.logical_or(first, second)
+        own_slot = jnp.where(either, j, own_slot)
+        owned = jnp.where(either, 1, owned)
+        role = jnp.where(second, 1, role)
     is_owner = owned == 1
+    owned_block = jnp.where(role == 0, d, CORES * x + (1 - core))
 
     def remote(src, dst, send, recv, dd, ff):
         return pltpu.make_async_remote_copy(
@@ -101,31 +108,39 @@
     for rel, stage in order:
         own_copy(rel, stage).start()
 
-    for step in range(1, groups):
-        greet((d + step) % groups, f)
-    for step in range(1, y_size):
-        greet(d, (y + step) % y_size * z_size + z)
-    for step in range(1, z_size):
-        greet(d, y * z_size + (z + step) % z_size)
-    for j in range(mats):
-
-        @pl.when(f != owners[j])
-        def _():
-            greet(d, owners[j])
-
-    @pl.when(is_owner)
-    def _():
-        def one(step, carry):
-            greet(d, (f + step) % shards)
-            return carry
-
-        lax.fori_loop(1, shards, one, 0)
-
-    pl.semaphore_wait(
-        barrier,
-        (groups - 1) + (y_size - 1) + (z_size - 1) + mats - owned + owned * (shards - 1),
-    )
-
+    def at_y(step):
+        return d, (y + step) % y_size * z_size + z
+
+    def at_low(step):
+        return d, y * z_size + zh * z_low + (zl + step) % z_low
+
+    def at_high(step):
+        return d, y * z_size + (zh + step) % z_high * z_low + zl
+
+    def at_x(step):
+        return CORES * ((x + step) % RING) + core, f
+
+    greet(sibling, f)
+    for size, where in ((RING, at_x), (y_size, at_y), (z_low, at_low), (z_high, at_high)):
+        for step in range(1, size):
+            greet(*where(step))
+    pl.semaphore_wait(barrier, 1 + (RING - 1) + (y_size - 1) + (z_low - 1) + (z_high - 1))
+
+    relays = ((z_high, at_high), (y_size, at_y), (2, lambda step: (sibling, f)))
+
+    def tell(stage):
+        size, where = relays[stage]
+        for step in range(1, size):
+            dd, ff = where(step)
+            pl.semaphore_signal(
+                known.at[stage], inc=1, device_id=(dd, ff),
+                device_id_type=pl.DeviceIdType.MESH,
+            )
+
+    def hear(stage):
+        pl.semaphore_wait(known.at[stage], relays[stage][0] - 1)
+
+    tell(0)
     for rel, stage in order:
         sib_copy(rel, stage).start()
 
@@ -203,13 +218,18 @@
                 ).astype(BF16)
             near_copy(way, quarter).start()
 
-    slot_here = z * y_size + y
+    odd = z % CORES
+    slot_here = z // CORES * y_size + y
 
     def in_copy(j):
         return remote(
             block(comb, 3 * mats + j), block(rows, slot_here),
-            in_send.at[j], in_recv.at[z], d, owners[j],
-        )
+            in_send.at[j], in_recv.at[z // CORES],
+            jnp.where(odd == 0, d, sibling), owners[j],
+        )
+
+    def stays(j):
+        return jnp.logical_and(f == owners[j], odd == 0)
 
     def combine(stage):
         arrived(3, stage)
@@ -228,22 +248,28 @@
                 )
                 comb[pl.ds((3 * mats + j) * height, height), :] = value.astype(BF16)
 
-                @pl.when(f != owners[j])
+                @pl.when(jnp.logical_not(stays(j)))
                 def _():
                     in_copy(j).start()
 
-                @pl.when(f == owners[j])
+                @pl.when(stays(j))
                 def _():
                     pltpu.make_async_copy(
-                        block(comb, 3 * mats + j), block(rows, slot_here), in_recv.at[z]
+                        block(comb, 3 * mats + j), block(rows, slot_here),
+                        in_recv.at[z // CORES],
                     ).start()
 
     sq_acc[...] = jnp.zeros_like(sq_acc)
     send_far(0)
+    hear(0)
+    tell(1)
     send_near(0)
+    hear(1)
+    tell(2)
     send_far(1)
     send_merged(0)
     send_near(1)
+    hear(2)
     combine(0)
     send_merged(1)
     combine(1)
@@ -269,48 +295,63 @@
 
     band = y_size * height
 
-    def near_z(step):
-        shift = jnp.where(step % 2 == 1, (step + 1) // 2, z_size - step // 2)
-        return (z + shift) % z_size
+    def near_band(step):
+        shift = jnp.where(step % 2 == 1, (step + 1) // 2, bands - step // 2)
+        return (z // CORES + shift) % bands
+
+    swap = remote(gram, gram_in, swap_send, swap_recv, sibling, f)
 
     @pl.when(is_owner)
     def _():
         gram[...] = jnp.zeros_like(gram)
 
         def one(step, carry):
-            zz = near_z(step)
-            here = rows.at[pl.ds(zz * band, band)]
-            pltpu.make_async_copy(here, here, in_recv.at[zz]).wait()
+            index = near_band(step)
+            here = rows.at[pl.ds(index * band, band)]
+            pltpu.make_async_copy(here, here, in_recv.at[index]).wait()
             part = here[...]
             gram[...] += lax.dot_general(
                 part, part, (((0,), (0,)), ((), ())), preferred_element_type=F32
             )
             return carry
 
-        lax.fori_loop(0, z_size, one, 0)
+        lax.fori_loop(0, bands, one, 0)
+        swap.start()
 
     for stage in (0, 1):
         for way in (0, 1):
             ag_copy(way, 2 * stage + way).wait_recv()
             agf_copy(way, stage).start()
 
-    def out_copy(y_to, z_to):
-        slot = z_to * y_size + y_to
+    def out_place(index, y_to):
+        return y_to * z_size + CORES * index + role
+
+    def out_stays(index, y_to):
+        return jnp.logical_and(role == 0, out_place(index, y_to) == f)
+
+    def out_copy(index, y_to):
+        slot = index * y_size + y_to
         return remote(
             block(done, slot), block(out_ref, own_slot),
-            out_send.at[slot], out_recv.at[own_slot], d, y_to * z_size + z_to,
+            out_send.at[slot], out_recv.at[own_slot],
+            owned_block, out_place(index, y_to),
         )
 
     @pl.when(is_owner)
     def _():
         row_id = lax.broadcasted_iota(jnp.int32, (width, width), 0)
         col_id = lax.broadcasted_iota(jnp.int32, (width, width), 1)
-        trace = jnp.sum(jnp.where(row_id == col_id, gram[...], 0.0), axis=0, keepdims=True)
+        swap.wait_recv()
+        gram_in[...] += gram[...]
+        swap.wait_send()
+        trace = jnp.sum(
+            jnp.where(row_id == col_id, gram_in[...], 0.0), axis=0, keepdims=True
+        )
         trace = jnp.sum(trace, axis=1, keepdims=True)
         scale = 1.0 / (jnp.sqrt(trace) + 1e-07)
         dot = lambda a, b: jnp.dot(a[...], b[...], preferred_element_type=F32)
 
-        gram[...] = gram[...] * scale * scale
+        gram[...] = gram_in[...] * scale * scale
         gram_b[...] = gram[...].astype(BF16)
         for lin, lin_b in ((lin0, lin0_b), (lin1, lin1_b)):
             lin[...] = COEF_B * gram[...] + COEF_C * dot(gram_b, gram_b)
@@ -328,28 +369,28 @@
         gram_b[...] = (whole * scale).astype(BF16)
 
         def one(step, carry):
-            zz = near_z(z_size - 1 - step)
-            at = pl.ds(zz * band, band)
+            index = near_band(bands - 1 - step)
+            at = pl.ds(index * band, band)
             done[at, :] = jnp.dot(
                 rows[at, :], gram_b[...], preferred_element_type=F32
             ).astype(BF16)
             for y_to in range(y_size):
-                here = y_to * z_size + zz == f
+                here = out_stays(index, y_to)
 
                 @pl.when(jnp.logical_not(here))
                 def _():
-                    out_copy(y_to, zz).start()
+                    out_copy(index, y_to).start()
 
                 @pl.when(here)
                 def _():
                     pltpu.make_async_copy(
-                        block(done, slot_here), block(out_ref, own_slot),
+                        block(done, index * y_size + y_to), block(out_ref, own_slot),
                         out_recv.at[own_slot],
                     ).start()
 
             return carry
 
-        lax.fori_loop(0, z_size, one, 0)
+        lax.fori_loop(0, bands, one, 0)
 
     for way in (0, 1):
         for quarter in range(4):
@@ -398,9 +439,11 @@
     )
     base = 0
     for size, place, where in (
-        (groups, d, lambda to: (to, f)),
-        (y_size, y, lambda to: (d, to * z_size + z)),
-        (z_size, z, lambda to: (d, y * z_size + to)),
+        (2, core, lambda step: (sibling, f)),
+        (RING, x, at_x),
+        (y_size, y, at_y),
+        (z_low, zl, at_low),
+        (z_high, zh, at_high),
     ):
         score[base + place] = tile
 
@@ -408,7 +451,7 @@
             return remote(
                 score.at[base + place], score.at[base + place],
                 red_send.at[base + step], red_recv.at[base + place],
-                *where((place + step) % size),
+                *where(step),
             )
 
         def red_wait(step, base=base, size=size, place=place):
@@ -454,18 +497,22 @@
             ag_copy(way, quarter).wait_send()
     for j in range(mats):
 
-        @pl.when(f != owners[j])
+        @pl.when(jnp.logical_not(stays(j)))
         def _():
             in_copy(j).wait_send()
 
     @pl.when(is_owner)
     def _():
-        def one(step, carry):
-            slot = (slot_here + step) % shards
-            out_copy(slot % y_size, slot // y_size).wait_send()
+        def one(index, carry):
+            for y_to in range(y_size):
+
+                @pl.when(jnp.logical_not(out_stays(index, y_to)))
+                def _():
+                    out_copy(index, y_to).wait_send()
+
             return carry
 
-        lax.fori_loop(1, shards, one, 0)
+        lax.fori_loop(0, bands, one, 0)
 
     for j in range(mats):
         here = block(out_ref, j)
@@ -479,12 +526,14 @@
     mats = matrices // groups
     y_size = 4 if shards == 64 else 2
     z_size = shards // y_size
-    sizes = (groups, y_size, z_size, mats, height, width)
+    z_low = 4 if z_size == 16 else 2
+    sizes = (groups, y_size, z_size, z_low, mats, height, width)
     assert groups == CORES * RING
     block = lambda count: pltpu.VMEM((count * height, width), BF16)
     square = lambda dtype: pltpu.VMEM((width, width), dtype)
     dma = lambda *shape: pltpu.SemaphoreType.DMA(shape)
-    red = groups + y_size + z_size
+    red = CORES + RING + y_size + z_low + z_size // z_low
+    held = shards // CORES
     finished, new_weights = pl.pallas_call(
         functools.partial(kernel, sizes),
         out_shape=(
@@ -499,16 +548,17 @@
         ),
         scratch_shapes=[
             block(RING * mats), block(RING * mats), block(mats), block(2 * mats),
-            block(mats), block(2 * mats), block(RING * mats), block(shards), block(shards),
-            square(F32), square(F32), square(F32), square(F32),
-            square(BF16), square(BF16), square(BF16), square(BF16),
+            block(mats), block(2 * mats), block(RING * mats), block(held), block(held),
+            *[square(F32)] * 5,
+            *[square(BF16)] * 4,
             pltpu.VMEM((red, 8, 128), F32), pltpu.VMEM((8, width), F32),
             dma(4, 2), dma(4, 2), dma(4, 2), dma(4), dma(4), dma(2, 4), dma(2, 4),
-            dma(2, 4), dma(2, 4), dma(2, 2), dma(2, 2), dma(mats), dma(z_size),
-            dma(shards), dma(mats), dma(red), dma(red),
+            dma(2, 4), dma(2, 4), dma(2, 2), dma(2, 2), dma(mats), dma(z_size // CORES),
+            dma(held), dma(mats), dma(red), dma(red), pltpu.SemaphoreType.DMA,
+            pltpu.SemaphoreType.DMA, pltpu.SemaphoreType.REGULAR((3,)),
         ],
         compiler_params=pltpu.CompilerParams(
-            collective_id=0, has_side_effects=True, vmem_limit_bytes=48 * 2**20
+            collective_id=0, has_side_effects=True, vmem_limit_bytes=60 * 2**20
         ),
         cost_estimate=pl.CostEstimate(
             flops=20 * 10**9, bytes_accessed=8 * 2**20, transcendentals=0

time: 133 us -> 130 us (0.977)
  the two profiles are of different devices: /device:TPU:1 before, /device:TPU:25 now
where the time goes in v2:
time: 130 us
  Pallas kernels  126 us (97%)
  other arithmetic  2.16 us (2%)
    pallas_call x1, Pallas kernels, body(): pl.pallas_call(functools.partial(kernel, sizes), out_shape=(jax.ShapeDtyp...  126 us

profile of v2, /device:TPU:25, one launch (start us, length us, event | category | flops | bytes accessed | tf_op | source)
XLA Modules:
  0.0 130.1 jit_solution(7667066687424356365)
XLA Ops:
  0.6 126.2 %shard_map.59 = (bf16[512,512]{1,0:T(8,128)(2,1)}, f32[1,128]{1,0:T(1,128)}) custom-call(s32[64]{0:T(128)} %counts_ref.1, s32[8]{0:T(128)} %ids_ref.1, f32[8]{0:T(128)} %weights_ref.1, bf16[4096,512]{1,0:T(8,128)(2,1)} %bitcast.5), custom_call_target="tpu_custom_call" | custom-call | flops 20000000000 | bytes 8388608 | tf_op jit(solution)/shard_map/pallas_call | solution.py:537
  126.8 1.1 slice_bitcast_fusion
  127.9 2.2 %convert_multiply_fusion = f32[512,512]{1,0:T(8,128)} fusion(bf16[512,512]{1,0:T(8,128)(2,1)} %get-tuple-element.4), kind=kLoop, calls=%fused_computation | loop fusion | flops 524288 | bytes 1572864 | tf_op jit(solution)/shard_map/mul | solution.py:568

commit v3 on v2

--- a/solution.py
+++ b/solution.py
@@ -22,10 +22,8 @@
 def owner_position(slot, core, y_size, z_size):
     if y_size * z_size != 64:
         return CORES * slot + core
-    quad, half = slot % 4, slot // 4
-    z_pos = 4 * quad + 2 * half + core
-    y_pos = (quad + ((0, 2), (1, 0))[half][core]) % 4
-    return y_pos * z_size + z_pos
+    z_pos = slot % 4 + 4 * (slot // 4) + 8 * core
+    return slot % 4 * z_size + z_pos
 
 
 def kernel(
@@ -35,7 +33,7 @@
     own, sib, far_out, near_out, far_in, near_in, comb, rows, done,
     gram, gram_in, term, lin0, lin1, gram_b, term_b, lin0_b, lin1_b, score, sq_acc,
     own_sem, sib_send, sib_recv, far_send, far_recv, near_send, near_recv,
-    ag_send, ag_recv, agf_send, agf_recv, in_send, in_recv, out_send, out_recv,
+    ag_send, ag_recv, in_send, in_recv, out_send, out_recv,
     red_send, red_recv, swap_send, swap_recv, known,
 ):
     groups, y_size, z_size, z_low, mats, height, width = sizes
@@ -57,12 +55,11 @@
             owner_position(j, 1, y_size, z_size),
         )
 
-    owners = [owner(j, core) for j in range(mats)]
     own_slot = jnp.int32(0)
     owned = jnp.int32(0)
     role = jnp.int32(0)
     for j in range(mats):
-        first, second = f == owners[j], f == owner(j, 1 - core)
+        first, second = f == owner(j, core), f == owner(j, 1 - core)
         either = jnp.logical_or(first, second)
         own_slot = jnp.where(either, j, own_slot)
         owned = jnp.where(either, 1, owned)
@@ -225,11 +222,11 @@
         return remote(
             block(comb, 3 * mats + j), block(rows, slot_here),
             in_send.at[j], in_recv.at[z // CORES],
-            jnp.where(odd == 0, d, sibling), owners[j],
+            jnp.where(odd == 0, d, sibling), owner(j, core),
         )
 
     def stays(j):
-        return jnp.logical_and(f == owners[j], odd == 0)
+        return jnp.logical_and(f == owner(j, core), odd == 0)
 
     def combine(stage):
         arrived(3, stage)
@@ -247,17 +244,31 @@
                     (value * value).reshape(height // 8, 8, width), axis=0
                 )
                 comb[pl.ds((3 * mats + j) * height, height), :] = value.astype(BF16)
-
-                @pl.when(jnp.logical_not(stays(j)))
-                def _():
-                    in_copy(j).start()
-
-                @pl.when(stays(j))
-                def _():
-                    pltpu.make_async_copy(
-                        block(comb, 3 * mats + j), block(rows, slot_here),
-                        in_recv.at[z // CORES],
-                    ).start()
+        for i in range(half):
+            j = half * stage + (i + z + y) % half
+
+            @pl.when(jnp.logical_not(stays(j)))
+            def _():
+                in_copy(j).start()
+
+            @pl.when(stays(j))
+            def _():
+                pltpu.make_async_copy(
+                    block(comb, 3 * mats + j), block(rows, slot_here),
+                    in_recv.at[z // CORES],
+                ).start()
+
+    def ag_copy(step, stage):
+        first = half * stage
+        return remote(
+            block(comb, 3 * mats + first, half),
+            block(comb, (3, 2, 0, 1)[step] * mats + first, half),
+            ag_send.at[step, stage], ag_recv.at[step, stage], *at_x(step),
+        )
+
+    def gather(stage):
+        for step in range(1, RING):
+            ag_copy(step, stage).start()
 
     sq_acc[...] = jnp.zeros_like(sq_acc)
     send_far(0)
@@ -272,26 +283,9 @@
     hear(2)
     combine(0)
     send_merged(1)
+    gather(0)
     combine(1)
-
-    def ag_copy(way, quarter):
-        first = quarter * pair
-        return remote(
-            block(comb, 3 * mats + first, pair),
-            block(comb, (2, 1)[way] * mats + first, pair),
-            ag_send.at[way, quarter], ag_recv.at[way, quarter], (plus, minus)[way], f,
-        )
-
-    def agf_copy(way, stage):
-        first = (2 * stage + way) * pair
-        return remote(
-            block(comb, (2, 1)[way] * mats + first, pair), block(comb, first, pair),
-            agf_send.at[way, stage], agf_recv.at[way, stage], (plus, minus)[way], f,
-        )
-
-    for quarter in range(4):
-        for way in (0, 1):
-            ag_copy(way, quarter).start()
+    gather(1)
 
     band = y_size * height
 
@@ -317,11 +311,6 @@
 
         lax.fori_loop(0, bands, one, 0)
         swap.start()
-
-    for stage in (0, 1):
-        for way in (0, 1):
-            ag_copy(way, 2 * stage + way).wait_recv()
-            agf_copy(way, stage).start()
 
     def out_place(index, y_to):
         return y_to * z_size + CORES * index + role
@@ -392,12 +381,9 @@
 
         lax.fori_loop(0, bands, one, 0)
 
-    for way in (0, 1):
-        for quarter in range(4):
-            if quarter % 2 != way:
-                ag_copy(way, quarter).wait_recv()
-        for stage in (0, 1):
-            agf_copy(way, stage).wait_recv()
+    for stage in (0, 1):
+        for step in range(1, RING):
+            ag_copy(step, stage).wait_recv()
 
     fold = lambda value: jnp.sum(value.reshape(height // 8, 8, width), axis=0)
 
@@ -491,10 +477,11 @@
     for way in (0, 1):
         for stage in (0, 1):
             far_copy(way, stage).wait_send()
-            agf_copy(way, stage).wait_send()
         for quarter in range(4):
             near_copy(way, quarter).wait_send()
-            ag_copy(way, quarter).wait_send()
+    for stage in (0, 1):
+        for step in range(1, RING):
+            ag_copy(step, stage).wait_send()
     for j in range(mats):
 
         @pl.when(jnp.logical_not(stays(j)))
@@ -553,7 +540,7 @@
             *[square(BF16)] * 4,
             pltpu.VMEM((red, 8, 128), F32), pltpu.VMEM((8, width), F32),
             dma(4, 2), dma(4, 2), dma(4, 2), dma(4), dma(4), dma(2, 4), dma(2, 4),
-            dma(2, 4), dma(2, 4), dma(2, 2), dma(2, 2), dma(mats), dma(z_size // CORES),
+            dma(4, 2), dma(4, 2), dma(mats), dma(z_size // CORES),
             dma(held), dma(mats), dma(red), dma(red), pltpu.SemaphoreType.DMA,
             pltpu.SemaphoreType.DMA, pltpu.SemaphoreType.REGULAR((3,)),
         ],

time: 130 us -> 117 us (0.900)
  the two profiles are of different devices: /device:TPU:25 before, /device:TPU:1 now
where the time goes in v3:
time: 117 us; the launch traced here: 116 us
  Pallas kernels  112 us (96%)
  other arithmetic  2.16 us (2%)
    pallas_call x1, Pallas kernels, body(): pl.pallas_call(functools.partial(kernel, sizes), out_shape=(jax.ShapeDtyp...  112 us

profile of v3, /device:TPU:1, one launch (start us, length us, event | category | flops | bytes accessed | tf_op | source)
XLA Modules:
  0.0 115.7 jit_solution(517310299806654358)
XLA Ops:
  0.6 111.8 %shard_map.59 = (bf16[512,512]{1,0:T(8,128)(2,1)}, f32[1,128]{1,0:T(1,128)}) custom-call(s32[64]{0:T(128)} %counts_ref.1, s32[8]{0:T(128)} %ids_ref.1, f32[8]{0:T(128)} %weights_ref.1, bf16[4096,512]{1,0:T(8,128)(2,1)} %bitcast.5), custom_call_target="tpu_custom_call" | custom-call | flops 20000000000 | bytes 8388608 | tf_op jit(solution)/shard_map/pallas_call | solution.py:524
  112.4 1.1 slice_bitcast_fusion
  113.5 2.2 %convert_multiply_fusion = f32[512,512]{1,0:T(8,128)} fusion(bf16[512,512]{1,0:T(8,128)(2,1)} %get-tuple-element.4), kind=kLoop, calls=%fused_computation | loop fusion | flops 524288 | bytes 1572864 | tf_op jit(solution)/shard_map/mul | solution.py:555

commit v4 on v3

--- a/solution.py
+++ b/solution.py
@@ -19,22 +19,15 @@
 RING = 4
 
 
-def owner_position(slot, core, y_size, z_size):
-    if y_size * z_size != 64:
-        return CORES * slot + core
-    z_pos = slot % 4 + 4 * (slot // 4) + 8 * core
-    return slot % 4 * z_size + z_pos
-
-
 def kernel(
     sizes,
     counts_ref, ids_ref, weights_ref, grads_ref,
     out_ref, new_ref,
-    own, sib, far_out, near_out, far_in, near_in, comb, rows, done,
+    own, sib, far_out, near_out, far_in, near_in, comb, rows, done, relay,
     gram, gram_in, term, lin0, lin1, gram_b, term_b, lin0_b, lin1_b, score, sq_acc,
     own_sem, sib_send, sib_recv, far_send, far_recv, near_send, near_recv,
     ag_send, ag_recv, in_send, in_recv, out_send, out_recv,
-    red_send, red_recv, swap_send, swap_recv, known,
+    relay_recv, pass_send, red_send, red_recv, swap_send, swap_recv, known,
 ):
     groups, y_size, z_size, z_low, mats, height, width = sizes
     z_high = z_size // z_low
@@ -48,24 +41,14 @@
     sibling = CORES * x + (1 - core)
     ring = [(x + step) % RING for step in (2, 1, 3, 0)]
     plus, minus = CORES * ring[1] + core, CORES * ring[2] + core
-    def owner(j, of_core):
-        return jnp.where(
-            of_core == 0,
-            owner_position(j, 0, y_size, z_size),
-            owner_position(j, 1, y_size, z_size),
-        )
-
-    own_slot = jnp.int32(0)
-    owned = jnp.int32(0)
-    role = jnp.int32(0)
-    for j in range(mats):
-        first, second = f == owner(j, core), f == owner(j, 1 - core)
-        either = jnp.logical_or(first, second)
-        own_slot = jnp.where(either, j, own_slot)
-        owned = jnp.where(either, 1, owned)
-        role = jnp.where(second, 1, role)
-    is_owner = owned == 1
-    owned_block = jnp.where(role == 0, d, CORES * x + (1 - core))
+    own_slot, holder = z % mats, z // mats
+    is_owner = y == z % y_size
+    role = jnp.where(core == holder, 0, 1)
+    owned_block = CORES * x + holder
+    skew = (y + y_size - z % y_size) % y_size
+
+    def owner(j):
+        return j % y_size * z_size + j + mats * core
 
     def remote(src, dst, send, recv, dd, ff):
         return pltpu.make_async_remote_copy(
@@ -101,7 +84,7 @@
             sib_send.at[rel, stage], sib_recv.at[rel, stage], sibling, f,
         )
 
-    order = [(0, 0), (1, 0), (2, 0), (0, 1), (3, 0), (1, 1), (2, 1), (3, 1)]
+    order = [(0, 0), (1, 0), (2, 0), (3, 0), (0, 1), (1, 1), (2, 1), (3, 1)]
     for rel, stage in order:
         own_copy(rel, stage).start()
 
@@ -222,11 +205,11 @@
         return remote(
             block(comb, 3 * mats + j), block(rows, slot_here),
             in_send.at[j], in_recv.at[z // CORES],
-            jnp.where(odd == 0, d, sibling), owner(j, core),
+            jnp.where(odd == 0, d, sibling), owner(j),
         )
 
     def stays(j):
-        return jnp.logical_and(f == owner(j, core), odd == 0)
+        return jnp.logical_and(f == owner(j), odd == 0)
 
     def combine(stage):
         arrived(3, stage)
@@ -277,14 +260,14 @@
     send_near(0)
     hear(1)
     tell(2)
+    send_merged(0)
     send_far(1)
-    send_merged(0)
-    send_near(1)
     hear(2)
     combine(0)
+    send_near(1)
     send_merged(1)
+    combine(1)
     gather(0)
-    combine(1)
     gather(1)
 
     band = y_size * height
@@ -312,11 +295,115 @@
         lax.fori_loop(0, bands, one, 0)
         swap.start()
 
+    for stage in (0, 1):
+        for step in range(1, RING):
+            ag_copy(step, stage).wait_recv()
+
+    fold = lambda value: jnp.sum(value.reshape(height // 8, 8, width), axis=0)
+
+    def align(index, carry):
+        rel, j = index // mats, index % mats
+        step = jnp.where(rel == 0, 2, jnp.where(rel == 1, 1, jnp.where(rel == 2, 3, 0)))
+        matrix = mats * (CORES * ((x + step) % RING) + core) + j
+        kept = jnp.where(f * height < counts_ref[matrix], 1.0, 0.0)
+        at = pl.ds(index * height, height)
+        mine, other = own[at, :].astype(F32), sib[at, :].astype(F32)
+        both = comb[at, :].astype(F32)
+        return (
+            carry[0] + fold(mine * both),
+            carry[1] + fold(other * both),
+            carry[2] + kept * fold(mine * mine),
+            carry[3] + kept * fold(other * other),
+        )
+
+    empty = jnp.zeros((8, width), F32)
+    sums = lax.fori_loop(0, RING * mats, align, (empty,) * 4)
+    sums = [
+        jnp.sum(jnp.sum(value, axis=0, keepdims=True), axis=1, keepdims=True)
+        for value in (*sums, sq_acc[...])
+    ]
+    sub = lax.broadcasted_iota(jnp.int32, (8, 128), 0)
+    lane = lax.broadcasted_iota(jnp.int32, (8, 128), 1)
+
+    def by_group(mine, other):
+        return jnp.where(sub == d, mine, jnp.where(sub == sibling, other, 0.0))
+
+    tile = jnp.where(
+        lane == 0,
+        by_group(sums[0], sums[1]),
+        jnp.where(
+            lane == 1,
+            by_group(sums[2], sums[3]),
+            jnp.where(lane == 2, sums[4], 0.0),
+        ),
+    )
+    def at_skew(z_to):
+        return d, (z_to + skew) % y_size * z_size + z_to
+
+    stages = (
+        (y_size, y, at_y),
+        (z_low, zl, lambda step: at_skew(zh * z_low + (zl + step) % z_low)),
+        (z_high, zh, lambda step: at_skew((zh + step) % z_high * z_low + zl)),
+        (CORES, core, lambda step: (sibling, f)),
+        (RING, x, at_x),
+    )
+    bases = [sum(size for size, _, _ in stages[:stage]) for stage in range(6)]
+    last = bases[5]
+
+    def red_copy(stage, step):
+        size, place, where = stages[stage]
+        mine = score.at[bases[stage] + place]
+        return remote(
+            mine, mine, red_send.at[bases[stage] + step],
+            red_recv.at[bases[stage] + place], *where(step),
+        )
+
+    def to_owner(step):
+        return (y + step) % y_size == z % y_size
+
+    def last_copy():
+        return remote(
+            score.at[last], score.at[last], red_send.at[last], red_recv.at[last],
+            d, z % y_size * z_size + z,
+        )
+
+    def hand_in(stage, value):
+        size, place, _ = stages[stage]
+        score[bases[stage] + place] = value
+        for step in range(1, size):
+            if stage == 0:
+
+                @pl.when(jnp.logical_not(to_owner(step)))
+                def _():
+                    red_copy(stage, step).start()
+
+            else:
+                red_copy(stage, step).start()
+
+    def summed(stage):
+        size, place, _ = stages[stage]
+        for step in range(1, size):
+            slot = bases[stage] + (place + step) % size
+            pltpu.make_async_copy(score.at[slot], score.at[slot], red_recv.at[slot]).wait()
+        value = score[bases[stage]]
+        for i in range(1, size):
+            value = value + score[bases[stage] + i]
+        return value
+
+    hand_in(0, tile)
+
     def out_place(index, y_to):
         return y_to * z_size + CORES * index + role
 
     def out_stays(index, y_to):
         return jnp.logical_and(role == 0, out_place(index, y_to) == f)
+
+    def relay_copy(index, y_to):
+        slot = index * y_size + y_to
+        return remote(
+            block(done, slot), block(relay, index),
+            out_send.at[slot], relay_recv.at[index], d, y_to * z_size + z,
+        )
 
     def out_copy(index, y_to):
         slot = index * y_size + y_to
@@ -366,7 +453,11 @@
             for y_to in range(y_size):
                 here = out_stays(index, y_to)
 
-                @pl.when(jnp.logical_not(here))
+                @pl.when(y_to != y)
+                def _():
+                    relay_copy(index, y_to).start()
+
+                @pl.when(jnp.logical_and(y_to == y, jnp.logical_not(here)))
                 def _():
                     out_copy(index, y_to).start()
 
@@ -381,82 +472,49 @@
 
         lax.fori_loop(0, bands, one, 0)
 
-    for stage in (0, 1):
-        for step in range(1, RING):
-            ag_copy(step, stage).wait_recv()
-
-    fold = lambda value: jnp.sum(value.reshape(height // 8, 8, width), axis=0)
-
-    def align(index, carry):
-        rel, j = index // mats, index % mats
-        step = jnp.where(rel == 0, 2, jnp.where(rel == 1, 1, jnp.where(rel == 2, 3, 0)))
-        matrix = mats * (CORES * ((x + step) % RING) + core) + j
-        kept = jnp.where(f * height < counts_ref[matrix], 1.0, 0.0)
-        at = pl.ds(index * height, height)
-        mine, other = own[at, :].astype(F32), sib[at, :].astype(F32)
-        both = comb[at, :].astype(F32)
-        return (
-            carry[0] + fold(mine * both),
-            carry[1] + fold(other * both),
-            carry[2] + kept * fold(mine * mine),
-            carry[3] + kept * fold(other * other),
-        )
-
-    empty = jnp.zeros((8, width), F32)
-    sums = lax.fori_loop(0, RING * mats, align, (empty,) * 4)
-    sums = [
-        jnp.sum(jnp.sum(value, axis=0, keepdims=True), axis=1, keepdims=True)
-        for value in (*sums, sq_acc[...])
-    ]
-    sub = lax.broadcasted_iota(jnp.int32, (8, 128), 0)
-    lane = lax.broadcasted_iota(jnp.int32, (8, 128), 1)
-
-    def by_group(mine, other):
-        return jnp.where(sub == d, mine, jnp.where(sub == sibling, other, 0.0))
-
-    tile = jnp.where(
-        lane == 0,
-        by_group(sums[0], sums[1]),
-        jnp.where(
-            lane == 1,
-            by_group(sums[2], sums[3]),
-            jnp.where(lane == 2, sums[4], 0.0),
-        ),
-    )
-    base = 0
-    for size, place, where in (
-        (2, core, lambda step: (sibling, f)),
-        (RING, x, at_x),
-        (y_size, y, at_y),
-        (z_low, zl, at_low),
-        (z_high, zh, at_high),
-    ):
-        score[base + place] = tile
-
-        def red_copy(step, base=base, size=size, place=place, where=where):
-            return remote(
-                score.at[base + place], score.at[base + place],
-                red_send.at[base + step], red_recv.at[base + place],
-                *where(step),
-            )
-
-        def red_wait(step, base=base, size=size, place=place):
-            came = score.at[base + (place + step) % size]
-            pltpu.make_async_copy(
-                came, came, red_recv.at[base + (place + step) % size]
-            ).wait()
-
-        for step in range(1, size):
-            red_copy(step).start()
-        for step in range(1, size):
-            red_wait(step)
-        tile = score[base]
-        for i in range(1, size):
-            tile = tile + score[base + i]
-        for step in range(1, size):
-            red_copy(step).wait_send()
-        base += size
-
+    def pass_copy(index):
+        return remote(
+            block(relay, index), block(out_ref, own_slot),
+            pass_send.at[index], out_recv.at[own_slot],
+            owned_block, out_place(index, y),
+        )
+
+    @pl.when(jnp.logical_not(is_owner))
+    def _():
+        step = 0
+        for stage in range(5):
+            value = summed(stage)
+            if stage == 4:
+                score[last] = value
+                break
+            hand_in(stage + 1, value)
+            for _ in range(bands // 4):
+                index = near_band(bands - 1 - step)
+                step += 1
+                here = block(relay, index)
+                pltpu.make_async_copy(here, here, relay_recv.at[index]).wait()
+                stay = out_stays(index, y)
+
+                @pl.when(jnp.logical_not(stay))
+                def _():
+                    pass_copy(index).start()
+
+                @pl.when(stay)
+                def _():
+                    pltpu.make_async_copy(
+                        block(relay, index), block(out_ref, own_slot),
+                        out_recv.at[own_slot],
+                    ).start()
+
+    @pl.when(skew == 1)
+    def _():
+        last_copy().start()
+
+    @pl.when(is_owner)
+    def _():
+        last_copy().wait_recv()
+
+    tile = score[last]
     id_col = jnp.zeros((8, 128), jnp.int32)
     weight_row = jnp.zeros((1, 128), F32)
     for g in range(groups):
@@ -488,6 +546,16 @@
         def _():
             in_copy(j).wait_send()
 
+    for step in range(1, y_size):
+
+        @pl.when(jnp.logical_not(to_owner(step)))
+        def _():
+            red_copy(0, step).wait_send()
+
+    @pl.when(skew == 1)
+    def _():
+        last_copy().wait_send()
+
     @pl.when(is_owner)
     def _():
         def one(index, carry):
@@ -496,6 +564,22 @@
                 @pl.when(jnp.logical_not(out_stays(index, y_to)))
                 def _():
                     out_copy(index, y_to).wait_send()
+
+            return carry
+
+        lax.fori_loop(0, bands, one, 0)
+
+    @pl.when(jnp.logical_not(is_owner))
+    def _():
+        for stage in range(1, 5):
+            for step in range(1, stages[stage][0]):
+                red_copy(stage, step).wait_send()
+
+        def one(index, carry):
+
+            @pl.when(jnp.logical_not(out_stays(index, y)))
+            def _():
+                pass_copy(index).wait_send()
 
             return carry
 
@@ -519,7 +603,8 @@
     block = lambda count: pltpu.VMEM((count * height, width), BF16)
     square = lambda dtype: pltpu.VMEM((width, width), dtype)
     dma = lambda *shape: pltpu.SemaphoreType.DMA(shape)
-    red = CORES + RING + y_size + z_low + z_size // z_low
+    red = CORES + RING + y_size + z_low + z_size // z_low + 1
+    assert z_size == CORES * mats and mats % y_size == 0
     held = shards // CORES
     finished, new_weights = pl.pallas_call(
         functools.partial(kernel, sizes),
@@ -535,13 +620,13 @@
         ),
         scratch_shapes=[
             block(RING * mats), block(RING * mats), block(mats), block(2 * mats),
-            block(mats), block(2 * mats), block(RING * mats), block(held), block(held),
+            block(mats), block(2 * mats), block(RING * mats), block(held), block(held), block(z_size // CORES),
             *[square(F32)] * 5,
             *[square(BF16)] * 4,
             pltpu.VMEM((red, 8, 128), F32), pltpu.VMEM((8, width), F32),
             dma(4, 2), dma(4, 2), dma(4, 2), dma(4), dma(4), dma(2, 4), dma(2, 4),
             dma(4, 2), dma(4, 2), dma(mats), dma(z_size // CORES),
-            dma(held), dma(mats), dma(red), dma(red), pltpu.SemaphoreType.DMA,
+            dma(held), dma(mats), dma(z_size // CORES), dma(z_size // CORES), dma(red), dma(red), pltpu.SemaphoreType.DMA,
             pltpu.SemaphoreType.DMA, pltpu.SemaphoreType.REGULAR((3,)),
         ],
         compiler_params=pltpu.CompilerParams(

time: 117 us -> 109 us (0.932)
  Pallas kernels: 112 us -> 105 us
    pallas_call x1, Pallas kernels: 112 us -> 105 us  [body(): pl.pallas_call(functools.partial(kernel, sizes), out_shape=(jax.ShapeDtyp...]
where the time goes in v4:
time: 109 us
  Pallas kernels  105 us (96%)
  other arithmetic  2.16 us (2%)
  local copies, waits for them, and re-layouts  1.11 us (1%)
    pallas_call x1, Pallas kernels, body(): pl.pallas_call(functools.partial(kernel, sizes), out_shape=(jax.ShapeDtyp...  105 us

profile of v4, /device:TPU:1, one launch (start us, length us, event | category | flops | bytes accessed | tf_op | source)
XLA Modules:
  0.0 108.5 jit_solution(14168100443846573805)
XLA Ops:
  0.6 104.6 %shard_map.59 = (bf16[512,512]{1,0:T(8,128)(2,1)}, f32[1,128]{1,0:T(1,128)}) custom-call(s32[64]{0:T(128)} %counts_ref.1, s32[8]{0:T(128)} %ids_ref.1, f32[8]{0:T(128)} %weights_ref.1, bf16[4096,512]{1,0:T(8,128)(2,1)} %bitcast.5), custom_call_target="tpu_custom_call" | custom-call | flops 20000000000 | bytes 8388608 | tf_op jit(solution)/shard_map/pallas_call | solution.py:609
  105.3 1.1 %slice_bitcast_fusion = f32[8]{0:T(128)} fusion(f32[1,128]{1,0:T(1,128)} %get-tuple-element.5), kind=kLoop, calls=%fused_computation.1 | loop fusion | bytes 64 | tf_op jit(solution)/shard_map/squeeze | solution.py:643
  106.4 2.2 %convert_multiply_fusion = f32[512,512]{1,0:T(8,128)} fusion(bf16[512,512]{1,0:T(8,128)(2,1)} %get-tuple-element.4), kind=kLoop, calls=%fused_computation | loop fusion | flops 524288 | bytes 1572864 | tf_op jit(solution)/shard_map/mul | solution.py:640

commit v5 on v4

--- a/solution.py
+++ b/solution.py
@@ -278,8 +278,7 @@
 
     swap = remote(gram, gram_in, swap_send, swap_recv, sibling, f)
 
-    @pl.when(is_owner)
-    def _():
+    def form_gram():
         gram[...] = jnp.zeros_like(gram)
 
         def one(step, carry):
@@ -294,6 +293,9 @@
 
         lax.fori_loop(0, bands, one, 0)
         swap.start()
+
+    early = own_slot < half
+    pl.when(jnp.logical_and(is_owner, early))(form_gram)
 
     for stage in (0, 1):
         for step in range(1, RING):
@@ -391,6 +393,7 @@
         return value
 
     hand_in(0, tile)
+    pl.when(jnp.logical_and(is_owner, jnp.logical_not(early)))(form_gram)
 
     def out_place(index, y_to):
         return y_to * z_size + CORES * index + role
@@ -481,34 +484,36 @@
 
     @pl.when(jnp.logical_not(is_owner))
     def _():
-        step = 0
-        for stage in range(5):
-            value = summed(stage)
-            if stage == 4:
-                score[last] = value
-                break
-            hand_in(stage + 1, value)
-            for _ in range(bands // 4):
-                index = near_band(bands - 1 - step)
-                step += 1
-                here = block(relay, index)
-                pltpu.make_async_copy(here, here, relay_recv.at[index]).wait()
-                stay = out_stays(index, y)
-
-                @pl.when(jnp.logical_not(stay))
-                def _():
-                    pass_copy(index).start()
-
-                @pl.when(stay)
-                def _():
-                    pltpu.make_async_copy(
-                        block(relay, index), block(out_ref, own_slot),
-                        out_recv.at[own_slot],
-                    ).start()
-
-    @pl.when(skew == 1)
-    def _():
-        last_copy().start()
+        def one(step, carry):
+            index = near_band(bands - 1 - step)
+            here = block(relay, index)
+            pltpu.make_async_copy(here, here, relay_recv.at[index]).wait()
+            stay = out_stays(index, y)
+
+            @pl.when(jnp.logical_not(stay))
+            def _():
+                pass_copy(index).start()
+
+            @pl.when(stay)
+            def _():
+                pltpu.make_async_copy(
+                    block(relay, index), block(out_ref, own_slot), out_recv.at[own_slot]
+                ).start()
+
+            return carry
+
+        for stage in (1, 2, 3):
+            hand_in(stage, summed(stage - 1))
+        lax.fori_loop(0, bands // 4, one, 0)
+        hand_in(4, summed(3))
+        lax.fori_loop(bands // 4, bands // 2, one, 0)
+        score[last] = summed(4)
+
+        @pl.when(skew == 1)
+        def _():
+            last_copy().start()
+
+        lax.fori_loop(bands // 2, bands, one, 0)
 
     @pl.when(is_owner)
     def _():

time: 109 us -> 105 us (0.963)
  Pallas kernels: 105 us -> 101 us
    pallas_call x1, Pallas kernels: 105 us -> 101 us  [body(): pl.pallas_call(functools.partial(kernel, sizes), out_shape=(jax.ShapeDtyp...]
where the time goes in v5:
time: 105 us
  Pallas kernels  101 us (96%)
  other arithmetic  2.16 us (2%)
  local copies, waits for them, and re-layouts  1.11 us (1%)
    pallas_call x1, Pallas kernels, body(): pl.pallas_call(functools.partial(kernel, sizes), out_shape=(jax.ShapeDtyp...  101 us
    mul x1, other arithmetic, body(): finished.reshape(mats, height, width).astype(F32)  2.16 us

profile of v5, /device:TPU:1, one launch (start us, length us, event | category | flops | bytes accessed | tf_op | source)
XLA Modules:
  0.0 105.2 jit_solution(16820782427021273332)
XLA Ops:
  0.6 101.3 %shard_map.59 = (bf16[512,512]{1,0:T(8,128)(2,1)}, f32[1,128]{1,0:T(1,128)}) custom-call(s32[64]{0:T(128)} %counts_ref.1, s32[8]{0:T(128)} %ids_ref.1, f32[8]{0:T(128)} %weights_ref.1, bf16[4096,512]{1,0:T(8,128)(2,1)} %bitcast.5), custom_call_target="tpu_custom_call" | custom-call | flops 20000000000 | bytes 8388608 | tf_op jit(solution)/shard_map/pallas_call | solution.py:614
  102.0 1.1 %slice_bitcast_fusion = f32[8]{0:T(128)} fusion(f32[1,128]{1,0:T(1,128)} %get-tuple-element.5), kind=kLoop, calls=%fused_computation.1 | loop fusion | bytes 64 | tf_op jit(solution)/shard_map/squeeze | solution.py:648
  103.1 2.2 %convert_multiply_fusion = f32[512,512]{1,0:T(8,128)} fusion(bf16[512,512]{1,0:T(8,128)(2,1)} %get-tuple-element.4), kind=kLoop, calls=%fused_computation | loop fusion | flops 524288 | bytes 1572864 | tf_op jit(solution)/shard_map/mul | solution.py:645

commit v6 on v5

--- a/solution.py
+++ b/solution.py
@@ -266,8 +266,8 @@
     combine(0)
     send_near(1)
     send_merged(1)
+    gather(0)
     combine(1)
-    gather(0)
     gather(1)
 
     band = y_size * height

time: 105 us -> 107 us (1.019)
  the two profiles are of different devices: /device:TPU:1 before, /device:TPU:22 now
where the time goes in v6:
time: 107 us
  Pallas kernels  103 us (96%)
  other arithmetic  2.16 us (2%)
  local copies, waits for them, and re-layouts  1.11 us (1%)
    pallas_call x1, Pallas kernels, body(): pl.pallas_call(functools.partial(kernel, sizes), out_shape=(jax.ShapeDtyp...  103 us
    mul x1, other arithmetic, body(): finished.reshape(mats, height, width).astype(F32)  2.16 us

profile of v6, /device:TPU:22, one launch (start us, length us, event | category | flops | bytes accessed | tf_op | source)
XLA Modules:
  0.0 106.7 jit_solution(4958195712199933107)
XLA Ops:
  0.6 102.8 %shard_map.59 = (bf16[512,512]{1,0:T(8,128)(2,1)}, f32[1,128]{1,0:T(1,128)}) custom-call(s32[64]{0:T(128)} %counts_ref.1, s32[8]{0:T(128)} %ids_ref.1, f32[8]{0:T(128)} %weights_ref.1, bf16[4096,512]{1,0:T(8,128)(2,1)} %bitcast.5), custom_call_target="tpu_custom_call" | custom-call | flops 20000000000 | bytes 8388608 | tf_op jit(solution)/shard_map/pallas_call | solution.py:614
  103.5 1.1 %slice_bitcast_fusion = f32[8]{0:T(128)} fusion(f32[1,128]{1,0:T(1,128)} %get-tuple-element.5), kind=kLoop, calls=%fused_computation.1 | loop fusion | bytes 64 | tf_op jit(solution)/shard_map/squeeze | solution.py:648
  104.6 2.2 %convert_multiply_fusion = f32[512,512]{1,0:T(8,128)} fusion(bf16[512,512]{1,0:T(8,128)(2,1)} %get-tuple-element.4), kind=kLoop, calls=%fused_computation | loop fusion | flops 524288 | bytes 1572864 | tf_op jit(solution)/shard_map/mul | solution.py:645
